TPU v7x, 32 devices: a whole 2x2x4 slice. The times are simulated.
32 devices in a mesh: mem: 2 (over x), fsdp: 16 (over z, y, core).
Axes of the slice: x: 2, y: 2, z: 4, core: 2. Of those that a mesh axis runs over, the one named last changes fastest.
Arguments:
- tokens: bfloat16 [32, 1024, 768], P('fsdp', 'mem'), may hold values from -6 to 6
- memory: bfloat16 [32, 256, 768], P('fsdp', 'mem'), may hold values from -6 to 6
- cotangent: bfloat16 [32, 1024, 768], P('fsdp', 'mem'), may hold values from -6 to 6
- text_len: int32 [32], P('fsdp'), may hold values from 1 to 1024, as said below
- mem_len: int32 [32], P('fsdp'), may hold values from 1 to 256
- image_flag: int32 [32], P('fsdp'), may hold values from 0 to 1
- self_qkv: bfloat16 [3, 768, 768], P(None, 'fsdp'), may hold values from -0.3125 to 0.3125
- self_out: bfloat16 [768, 768], P('fsdp'), may hold values from -0.875 to 0.875
- cross_qkv: bfloat16 [3, 768, 768], P(None, 'fsdp'), may hold values from -0.3125 to 0.3125
- cross_out: bfloat16 [768, 768], P('fsdp'), may hold values from -0.625 to 0.625
- w_in: bfloat16 [768, 3072], P('fsdp'), may hold values from -0.21875 to 0.21875
- w_out: bfloat16 [3072, 768], P('fsdp'), may hold values from -0.109375 to 0.109375
- b_in: bfloat16 [3072], P('fsdp'), may hold values from -3 to 3
- b_out: bfloat16 [768], P('fsdp'), may hold values from -2 to 2
- norm_gain: bfloat16 [3, 768], P(None, 'fsdp'), may hold values from 0.099609375 to 1.8984375
- norm_bias: bfloat16 [3, 768], P(None, 'fsdp'), may hold values from -2 to 2
Outputs:
- mixed: bfloat16 [32, 1024, 768], P('fsdp', 'mem')
- grad_tokens: float32 [32, 1024, 768], P('fsdp', 'mem')
- grad_memory: float32 [32, 256, 768], P('fsdp', 'mem')
- grad_self_qkv: float32 [3, 768, 768], P(None, 'fsdp')
- grad_self_out: float32 [768, 768], P('fsdp')
- grad_cross_qkv: float32 [3, 768, 768], P(None, 'fsdp')
- grad_cross_out: float32 [768, 768], P('fsdp')
- grad_w_in: float32 [768, 3072], P('fsdp')
- grad_w_out: float32 [3072, 768], P('fsdp')
- grad_b_in: float32 [3072], P('fsdp')
- grad_b_out: float32 [768], P('fsdp')
- grad_norm_gain: float32 [3, 768], P(None, 'fsdp')
- grad_norm_bias: float32 [3, 768], P(None, 'fsdp')
Inputs may be any that keep to these rules, and one draw needn't show every extreme that they name: In each aligned run of 2 sequences one has text_len 1024, mem_len 256 and image_flag 1.
All inputs are finite; a program needn't handle non-finite values.
Results may differ from a plain program's by a relative error of at most 0.029.
The roundings to bfloat16 on the way count: a program that leaves them out, or rounds other values in their place, can miss the bound.
Values may be sent and summed in bfloat16 or wider, within the bound.
A program may use at most 256 MiB of HBM per device.

v0:
```python
import jax
import jax.numpy as jnp
from jax import lax
from jax.sharding import PartitionSpec as P

HEAD_FEATURES = 64


EPSILON = 1e-05


def layer_norm(values, gain, shift):
    centre = values - jnp.mean(values, -1, keepdims=True)
    spread = jnp.mean(centre * centre, -1, keepdims=True)
    return centre * lax.rsqrt(spread + EPSILON) * gain + shift


def gelu_exact(values):
    return jax.nn.gelu(values, approximate=False)


def split_heads(values):
    return values.reshape(values.shape[0], values.shape[1], -1, HEAD_FEATURES).transpose(2, 0, 1, 3)


def merge_heads(values):
    return values.transpose(1, 2, 0, 3).reshape(values.shape[1], values.shape[2], -1)


def head_scores(query_matrix, key_matrix, allowed):
    logit_scores = jnp.einsum(
        "cti,cvi->ctv", query_matrix, key_matrix, preferred_element_type=jnp.float32
    ) * HEAD_FEATURES ** (-0.5)
    return jnp.where(allowed, logit_scores, -1000000000.0)


def attend(query_matrix, key_matrix, values, allowed):

    def one_head(parts):
        head_query_rows, head_key_rows, head_value_rows = parts
        logit_scores = head_scores(head_query_rows, head_key_rows, allowed)
        row_max = jnp.max(logit_scores, -1, keepdims=True)
        expo = jnp.exp(logit_scores - row_max)
        row_sum = jnp.sum(expo, -1, keepdims=True)
        reduced_probabilities = (expo / row_sum).astype(jnp.bfloat16)
        attention_output = jnp.einsum(
            "zqf,zfm->zqm",
            reduced_probabilities,
            head_value_rows,
            preferred_element_type=jnp.float32,
        )
        return (attention_output, row_max, row_sum)

    attention_output, row_max, row_sum = lax.map(
        one_head, (split_heads(query_matrix), split_heads(key_matrix), split_heads(values))
    )
    return (merge_heads(attention_output).astype(jnp.bfloat16), row_max, row_sum)


def attend_back(query_matrix, key_matrix, values, allowed, row_max, row_sum, grad_out):

    def one_head(parts):
        (
            head_query_rows,
            head_key_rows,
            head_value_rows,
            head_output_gradient,
            head_max,
            head_sum,
        ) = parts
        logit_scores = head_scores(head_query_rows, head_key_rows, allowed)
        probs = jnp.exp(logit_scores - head_max) / head_sum
        reduced_probabilities = probs.astype(jnp.bfloat16)
        probs_gradient = jnp.einsum(
            "cti,cvi->ctv",
            head_output_gradient,
            head_value_rows,
            preferred_element_type=jnp.float32,
        )
        delta_sum = jnp.sum(probs * probs_gradient, -1, keepdims=True)
        scores_gradient = (probs * (probs_gradient - delta_sum)).astype(jnp.bfloat16)
        d_query = jnp.einsum(
            "zqf,zfm->zqm", scores_gradient, head_key_rows, preferred_element_type=jnp.float32
        ) * HEAD_FEATURES ** (-0.5)
        d_keys = jnp.einsum(
            "pum,pug->pmg", scores_gradient, head_query_rows, preferred_element_type=jnp.float32
        ) * HEAD_FEATURES ** (-0.5)
        values_gradient = jnp.einsum(
            "pum,pug->pmg",
            reduced_probabilities,
            head_output_gradient,
            preferred_element_type=jnp.float32,
        )
        return (d_query, d_keys, values_gradient)

    d_query, d_keys, values_gradient = lax.map(
        one_head,
        (
            split_heads(query_matrix),
            split_heads(key_matrix),
            split_heads(values),
            split_heads(grad_out),
            row_max,
            row_sum,
        ),
    )
    return (merge_heads(d_query), merge_heads(d_keys), merge_heads(values_gradient))


def body(
    tokens,
    memory,
    cotangent,
    text_len,
    mem_len,
    image_flag,
    self_qkv,
    self_out,
    cross_qkv,
    cross_out,
    w_in,
    w_out,
    b_in,
    b_out,
    norm_gain,
    norm_bias,
):
    f32 = jnp.float32
    b16 = jnp.bfloat16
    seq_count, own_rows, width = tokens.shape
    offset = lax.axis_index("mem") * own_rows
    gathered = (
        lax.all_gather(self_qkv, "fsdp", axis=1, tiled=True),
        lax.all_gather(self_out, "fsdp", axis=0, tiled=True),
        lax.all_gather(cross_qkv, "fsdp", axis=1, tiled=True),
        lax.all_gather(cross_out, "fsdp", axis=0, tiled=True),
        lax.all_gather(w_in, "fsdp", axis=0, tiled=True),
        lax.all_gather(w_out, "fsdp", axis=0, tiled=True),
        lax.all_gather(b_in, "fsdp", axis=0, tiled=True),
        lax.all_gather(b_out, "fsdp", axis=0, tiled=True),
        lax.all_gather(norm_gain, "fsdp", axis=1, tiled=True),
        lax.all_gather(norm_bias, "fsdp", axis=1, tiled=True),
    )
    (
        self_w,
        self_proj,
        cross_w,
        cross_proj,
        inner_w,
        outer_w,
        inner_bias,
        outer_bias,
        gains,
        shifts,
    ) = gathered
    gains = gains.astype(f32)
    shifts = shifts.astype(f32)
    x0 = tokens.astype(f32)
    h1_full, norm0_back = jax.vjp(layer_norm, x0, gains[0], shifts[0])
    h1 = h1_full.astype(b16)
    qkv = jnp.einsum("srd,kde->ksre", h1, self_w, preferred_element_type=f32).astype(b16)
    keys_all, values_all = (
        lax.all_gather(qkv[1], "mem", axis=1, tiled=True),
        lax.all_gather(qkv[2], "mem", axis=1, tiled=True),
    )
    key_pos = jnp.arange(keys_all.shape[1], dtype=jnp.int32)
    query_pos = offset + jnp.arange(own_rows, dtype=jnp.int32)
    self_mask = (key_pos[None, None, :] <= query_pos[None, :, None]) & (
        key_pos[None, None, :] < text_len[:, None, None]
    )
    attended, self_max, self_sum = attend(qkv[0], keys_all, values_all, self_mask)
    x1 = x0 + jnp.einsum("srd,de->sre", attended, self_proj, preferred_element_type=f32)
    h2_full, norm1_back = jax.vjp(layer_norm, x1, gains[1], shifts[1])
    h2 = h2_full.astype(b16)
    cross_q = jnp.einsum("srd,de->sre", h2, cross_w[0], preferred_element_type=f32).astype(b16)
    memory_all = lax.all_gather(memory, "mem", axis=1, tiled=True)
    cross_kv = jnp.einsum(
        "snd,kde->ksne", memory_all, cross_w[1:], preferred_element_type=f32
    ).astype(b16)
    cross_keys, cross_values = (cross_kv[0], cross_kv[1])
    mem_pos = jnp.arange(cross_keys.shape[1], dtype=jnp.int32)
    cross_mask = mem_pos[None, None, :] < mem_len[:, None, None]
    crossed, cross_max, cross_sum = attend(cross_q, cross_keys, cross_values, cross_mask)
    flag = image_flag.astype(f32)[:, None, None]
    x2 = x1 + jnp.einsum("srd,de->sre", crossed, cross_proj, preferred_element_type=f32) * flag
    h3_full, norm2_back = jax.vjp(layer_norm, x2, gains[2], shifts[2])
    h3 = h3_full.astype(b16)
    pre = jnp.einsum("srd,df->srf", h3, inner_w, preferred_element_type=f32) + inner_bias.astype(
        f32
    )
    act_full, gelu_back = jax.vjp(gelu_exact, pre)
    act_low = act_full.astype(b16)
    attention_output = (
        x2
        + jnp.einsum("srf,fd->srd", act_low, outer_w, preferred_element_type=f32)
        + outer_bias.astype(f32)
    )
    mixed = attention_output.astype(b16)
    grad_top = cotangent.astype(f32)
    grad_low = grad_top.astype(b16)
    grad_outer_bias = jnp.sum(grad_low.astype(f32), (0, 1))
    grad_outer = jnp.einsum("srf,srd->fd", act_low, grad_low, preferred_element_type=f32)
    d_act = jnp.einsum("srd,fd->srf", grad_low, outer_w, preferred_element_type=f32)
    d_pre = gelu_back(d_act)[0].astype(b16)
    grad_inner_bias = jnp.sum(d_pre.astype(f32), (0, 1))
    grad_inner = jnp.einsum("srd,srf->df", h3, d_pre, preferred_element_type=f32)
    d_h3 = jnp.einsum("srf,df->srd", d_pre, inner_w, preferred_element_type=f32)
    d_x2, gain_two, shift_two = norm2_back(d_h3)
    grad_two = grad_top + d_x2
    grad_cross = (grad_two * flag).astype(b16)
    grad_cross_proj = jnp.einsum("srd,sre->de", crossed, grad_cross, preferred_element_type=f32)
    d_crossed = jnp.einsum(
        "sre,de->srd", grad_cross, cross_proj, preferred_element_type=f32
    ).astype(b16)
    d_cross_q, d_cross_k, d_cross_v = attend_back(
        cross_q, cross_keys, cross_values, cross_mask, cross_max, cross_sum, d_crossed
    )
    own_cross_k, own_cross_v = (
        lax.psum_scatter(
            d_cross_k.astype(jnp.bfloat16), "mem", scatter_dimension=1, tiled=True
        ).astype(jnp.float32),
        lax.psum_scatter(
            d_cross_v.astype(jnp.bfloat16), "mem", scatter_dimension=1, tiled=True
        ).astype(jnp.float32),
    )
    d_cross_kv = jnp.stack([own_cross_k, own_cross_v]).astype(b16)
    grad_cross_kv = jnp.einsum("snd,ksne->kde", memory, d_cross_kv, preferred_element_type=f32)
    grad_memory = jnp.einsum("ksne,kde->snd", d_cross_kv, cross_w[1:], preferred_element_type=f32)
    d_cross_low = d_cross_q.astype(b16)
    grad_cross_q = jnp.einsum("srd,sre->de", h2, d_cross_low, preferred_element_type=f32)
    d_h2 = jnp.einsum("sre,de->srd", d_cross_low, cross_w[0], preferred_element_type=f32)
    d_x1, gain_one, shift_one = norm1_back(d_h2)
    grad_one = grad_two + d_x1
    grad_cross_w = jnp.concatenate([grad_cross_q[None], grad_cross_kv], 0)
    grad_one_low = grad_one.astype(b16)
    grad_self_proj = jnp.einsum("srd,sre->de", attended, grad_one_low, preferred_element_type=f32)
    d_attended = jnp.einsum(
        "sre,de->srd", grad_one_low, self_proj, preferred_element_type=f32
    ).astype(b16)
    d_query, d_keys, values_gradient = attend_back(
        qkv[0], keys_all, values_all, self_mask, self_max, self_sum, d_attended
    )
    own_keys, own_values = (
        lax.psum_scatter(
            d_keys.astype(jnp.bfloat16), "mem", scatter_dimension=1, tiled=True
        ).astype(jnp.float32),
        lax.psum_scatter(
            values_gradient.astype(jnp.bfloat16), "mem", scatter_dimension=1, tiled=True
        ).astype(jnp.float32),
    )
    d_qkv = jnp.stack([d_query, own_keys, own_values]).astype(b16)
    grad_self_w = jnp.einsum("srd,ksre->kde", h1, d_qkv, preferred_element_type=f32)
    d_h1 = jnp.einsum("ksre,kde->srd", d_qkv, self_w, preferred_element_type=f32)
    d_x0, gain_zero, shift_zero = norm0_back(d_h1)
    grad_tokens = grad_one + d_x0
    gain_grads = jnp.stack([gain_zero, gain_one, gain_two])
    shift_grads = jnp.stack([shift_zero, shift_one, shift_two])
    full_grads = (
        grad_self_w,
        grad_self_proj,
        grad_cross_w,
        grad_cross_proj,
        grad_inner,
        grad_outer,
        grad_inner_bias,
        grad_outer_bias,
        gain_grads,
        shift_grads,
    )
    shards = (
        lax.psum_scatter(
            full_grads[0].astype(jnp.bfloat16), "fsdp", scatter_dimension=1, tiled=True
        ).astype(jnp.float32),
        lax.psum_scatter(
            full_grads[1].astype(jnp.bfloat16), "fsdp", scatter_dimension=0, tiled=True
        ).astype(jnp.float32),
        lax.psum_scatter(
            full_grads[2].astype(jnp.bfloat16), "fsdp", scatter_dimension=1, tiled=True
        ).astype(jnp.float32),
        lax.psum_scatter(
            full_grads[3].astype(jnp.bfloat16), "fsdp", scatter_dimension=0, tiled=True
        ).astype(jnp.float32),
        lax.psum_scatter(
            full_grads[4].astype(jnp.bfloat16), "fsdp", scatter_dimension=0, tiled=True
        ).astype(jnp.float32),
        lax.psum_scatter(
            full_grads[5].astype(jnp.bfloat16), "fsdp", scatter_dimension=0, tiled=True
        ).astype(jnp.float32),
        lax.psum_scatter(
            full_grads[6].astype(jnp.bfloat16), "fsdp", scatter_dimension=0, tiled=True
        ).astype(jnp.float32),
        lax.psum_scatter(
            full_grads[7].astype(jnp.bfloat16), "fsdp", scatter_dimension=0, tiled=True
        ).astype(jnp.float32),
        lax.psum_scatter(
            full_grads[8].astype(jnp.bfloat16), "fsdp", scatter_dimension=1, tiled=True
        ).astype(jnp.float32),
        lax.psum_scatter(
            full_grads[9].astype(jnp.bfloat16), "fsdp", scatter_dimension=1, tiled=True
        ).astype(jnp.float32),
    )
    totals = (
        lax.psum(shards[0].astype(jnp.bfloat16), "mem").astype(jnp.float32),
        lax.psum(shards[1].astype(jnp.bfloat16), "mem").astype(jnp.float32),
        lax.psum(shards[2].astype(jnp.bfloat16), "mem").astype(jnp.float32),
        lax.psum(shards[3].astype(jnp.bfloat16), "mem").astype(jnp.float32),
        lax.psum(shards[4].astype(jnp.bfloat16), "mem").astype(jnp.float32),
        lax.psum(shards[5].astype(jnp.bfloat16), "mem").astype(jnp.float32),
        lax.psum(shards[6].astype(jnp.bfloat16), "mem").astype(jnp.float32),
        lax.psum(shards[7].astype(jnp.bfloat16), "mem").astype(jnp.float32),
        lax.psum(shards[8].astype(jnp.bfloat16), "mem").astype(jnp.float32),
        lax.psum(shards[9].astype(jnp.bfloat16), "mem").astype(jnp.float32),
    )
    return (
        mixed,
        grad_tokens,
        grad_memory,
        totals[0],
        totals[1],
        totals[2],
        totals[3],
        totals[4],
        totals[5],
        totals[6],
        totals[7],
        totals[8],
        totals[9],
    )


def solution(mesh):
    placed = (
        P("fsdp", "mem", None),
        P("fsdp", "mem", None),
        P("fsdp", "mem", None),
        P("fsdp"),
        P("fsdp"),
        P("fsdp"),
        P(None, "fsdp", None),
        P("fsdp", None),
        P(None, "fsdp", None),
        P("fsdp", None),
        P("fsdp", None),
        P("fsdp", None),
        P("fsdp"),
        P("fsdp"),
        P(None, "fsdp"),
        P(None, "fsdp"),
    )
    return jax.shard_map(
        body,
        mesh=mesh,
        in_specs=placed,
        out_specs=(
            P("fsdp", "mem", None),
            P("fsdp", "mem", None),
            P("fsdp", "mem", None),
            P(None, "fsdp", None),
            P("fsdp", None),
            P(None, "fsdp", None),
            P("fsdp", None),
            P("fsdp", None),
            P("fsdp", None),
            P("fsdp"),
            P("fsdp"),
            P(None, "fsdp"),
            P(None, "fsdp"),
        ),
        check_vma=False,
    )
```

profile of v0, /device:TPU:0, one launch (start us, length us, event | category | flops | bytes accessed | tf_op | source)
XLA Modules:
  0.0 1468.5 jit_solution(1084119821501333818)
XLA Ops:
  8.7 23.4 %all-gather.2 = bf16[16,48,3]{1,2,0:T(4,128)(2,1)S(1)} all-gather(bf16[1,48,3]{1,2,0:T(4,128)(2,1)} %bitcast.450), channel_id=1, replica_groups=mesh['mem'=2,'fsdp'=16] {'fsdp'}, dimensions={0}, use_global_device_ids=true | all-gather | bytes 4896 | tf_op jit(solution)/shard_map/all_gather | solution.py:141
  32.2 17.8 %all-gather.3 = bf16[16,48,3]{1,2,0:T(4,128)(2,1)S(1)} all-gather(bf16[1,48,3]{1,2,0:T(4,128)(2,1)} %bitcast.451), channel_id=1, replica_groups=mesh['mem'=2,'fsdp'=16] {'fsdp'}, dimensions={0}, use_global_device_ids=true | all-gather | bytes 4896 | tf_op jit(solution)/shard_map/all_gather | solution.py:142
  53.1 7.2 all-gather.13.cloned.1.call-done
  60.3 6.3 convert_bitcast_fusion
  72.5 11.9 all_gather.46
  86.0 32.4 %all-reduce = bf16[3072]{0:T(1024)(128)(2,1)S(1)} all-reduce(bf16[3072]{0:T(1024)(128)(2,1)S(1)} %dynamic-update-slice), channel_id=1, replica_groups=mesh['mem'=2,'fsdp'=16] {'fsdp'}, use_global_device_ids=true, to_apply=%add | all-reduce | flops 3072 | bytes 12288
  121.8 3.2 fusion.145
  126.5 29.3 %all-gather.25.cloned.1.call-done = bf16[1,2,1024,768]{3,2,0,1:T(8,128)(2,1)} async-done(((bf16[1,2,512,768]{3,2,0,1:T(8,128)(2,1)}), bf16[1,2,1024,768]{3,2,0,1:T(8,128)(2,1)}) %all-gather.25.cloned.1.call-update) | async-done | bytes 3145744 | tf_op jit(solution)/shard_map/all_gather | solution.py:163
  155.8 4.6 copy.166
  160.4 4.1 copy.169
  164.5 38.2 %all-gather.27.cloned.1.call-done = bf16[1,2,1024,768]{3,2,0,1:T(8,128)(2,1)} async-done(((bf16[1,2,512,768]{3,2,0,1:T(8,128)(2,1)}), bf16[1,2,1024,768]{3,2,0,1:T(8,128)(2,1)}) %all-gather.27.cloned.1.call-update) | async-done | bytes 3145744 | tf_op jit(solution)/shard_map/all_gather | solution.py:164
  202.7 4.6 copy.167
  207.4 4.0 copy.170
  212.7 81.5 %while.60 = (s32[]{:T(128)}, bf16[12,2,512,64]{2,3,0,1:T(8,128)(2,1)}, f32[12,2,512,1]{2,1,3,0:T(2,128)S(1)}, f32[12,2,512,1]{2,1,3,0:T(2,128)S(1)}, bf16[12,2,5...) while((s32[]{:T(128)}, ...), condition=%wide.region_5.6_spmd.clone, body=%wide.region_2.5_spmd.clone.sunk | while | flops 284162048 | bytes 15120489 | solution.py:54
  216.3 3.3 fusion.235
  223.1 3.3 fusion.235
  229.9 3.3 fusion.235
  236.7 3.3 fusion.235
  243.5 3.3 fusion.235
  250.2 3.3 fusion.235
  257.0 3.3 fusion.235
  263.8 3.3 fusion.235
  270.6 3.3 fusion.235
  277.4 3.3 fusion.235
  284.2 3.3 fusion.235
  291.0 3.3 fusion.235
  295.5 3.8 fusion.179
  300.0 4.0 convolution_convert_fusion.2
  310.8 40.4 %while.61 = (s32[]{:T(128)}, bf16[12,2,512,64]{2,3,0,1:T(8,128)(2,1)}, f32[12,2,512,1]{2,1,3,0:T(2,128)S(1)}, f32[12,2,512,1]{2,1,3,0:T(2,128)S(1)}, bf16[12,2,5...) while((s32[]{:T(128)}, ...), condition=%wide.region_11.12_spmd.clone, body=%wide.region_8.11_spmd.clone.sunk | while | flops 69204480 | bytes 3710057 | solution.py:54
  351.2 3.4 fusion.180
  356.8 15.6 %fusion.129 = (u8[512,3072]{1,0:T(8,128)(4,1)S(1)}, u8[512,3072]{1,0:T(8,128)(4,1)S(1)}, f32[2,512,3072]{2,1,0:T(8,128)}) fusion(f32[3072]{0:T(1024)S(1)} %convert_element_type.249, bf16[768,3072]{1,0:T(8,128)(2,1)} %all-gather.21.cloned.1.call-done, f32[2,512,768]{2,1,0:T(8,128)} %copy-done, f32[768]{0:T(1024)S(1)} %copy-done.42, f32[768]{0:T(1024)S(1)} %copy-done.38, ...), kind=kOutput, calls=%fused_computation.193 | convolution fusion | flops 4876664832 | bytes 23619584 | tf_op jit(solution)/shard_map/srd,df->srf/dot_general | solution.py:188
  372.4 31.9 %multiply_convert_fusion.2 = (bf16[2,512,3072]{2,1,0:T(8,128)(2,1)}, f32[2,512,3072]{2,1,0:T(8,128)}) fusion(f32[2,512,3072]{2,1,0:T(8,128)} %get-tuple-element.642, f32[3072]{0:T(1024)S(1)} %convert_element_type.249, u8[512,3072]{1,0:T(8,128)(4,1)S(1)} %get-tuple-element.498, u8[512,3072]{1,0:T(8,128)(4,1)S(1)} %get-tuple-element.497), kind=kLoop, calls=%fused_computation.127 | loop fusion | flops 223346688 | bytes 34615296 | tf_op jit(solution)/shard_map/convert_element_type | solution.py:192
  404.4 19.4 %fusion.181 = (bf16[3072]{0:T(1024)(128)(2,1)}, bf16[2,512,3072]{2,1,0:T(8,128)(2,1)}) fusion(f32[2,512,3072]{2,1,0:T(8,128)} %get-tuple-element.614, bf16[2,512,768]{2,1,0:T(8,128)(2,1)} %param.26, bf16[3072,768]{1,0:T(8,128)(2,1)} %all-gather.23.cloned.1.call-done, f32[2,512,3072]{2,1,0:T(8,128)} %get-tuple-element.642, f32[3072]{0:T(1024)S(1)} %convert_element_type.249), kind=kOutput, calls=%fused_computation.269 | convolution fusion | flops 4882166784 | bytes 37767168 | tf_op jit(solution)/shard_map/srd,fd->srf/dot_general | solution.py:203
  423.7 9.9 multiply_reduce_fusion.2
  444.3 100.5 %while.62 = (s32[]{:T(128)}, bf16[12,2,512,64]{2,3,0,1:T(8,128)(2,1)}, bf16[12,2,256,64]{2,3,0,1:T(8,128)(2,1)}, bf16[12,2,256,64]{2,3,0,1:T(8,128)(2,1)}, bf16[...) while((s32[]{:T(128)}, ...), condition=%wide.region_18.19_spmd.clone, body=%wide.region_16.18_spmd.clone.sunk | while | flops 170491392 | bytes 9148545 | solution.py:96
  544.8 5.9 fusion.172
  553.1 3.6 multiply_reduce_fusion.3
  570.1 142.8 %while.63 = (s32[]{:T(128)}, bf16[12,2,512,64]{2,3,0,1:T(8,128)(2,1)}, bf16[12,2,1024,64]{2,3,0,1:T(8,128)(2,1)}, bf16[12,2,1024,64]{2,3,0,1:T(8,128)(2,1)}, bf1...) while((s32[]{:T(128)}, ...), condition=%wide.region_23.24_spmd.clone, body=%wide.region_21.23_spmd.clone.sunk | while | flops 682818560 | bytes 36740252 | solution.py:96
  583.9 3.0 multiply_reduce_fusion.11
  712.9 4.7 copy.192
  717.7 4.7 copy.194
  722.5 3.2 copy.195
  725.7 4.3 fusion.148
  735.7 8.3 copy.206
  744.0 17.1 %reduce-scatter.15.cloned.1.call-done = bf16[2,512,768]{2,1,0:T(8,128)(2,1)} async-done(((bf16[2,1024,768]{2,1,0:T(8,128)(2,1)}), bf16[2,512,768]{2,1,0:T(8,128)(2,1)}) %reduce-scatter.15.cloned.1.call-update) | async-done | bytes 1572880 | tf_op jit(solution)/shard_map/reduce_scatter | solution.py:244
  761.1 45.6 %reduce-scatter.17.cloned.1.call-done = bf16[2,512,768]{2,1,0:T(8,128)(2,1)} async-done(((bf16[2,1024,768]{2,1,0:T(8,128)(2,1)}), bf16[2,512,768]{2,1,0:T(8,128)(2,1)}) %reduce-scatter.17.cloned.1.call-update) | async-done | bytes 1572880 | tf_op jit(solution)/shard_map/reduce_scatter | solution.py:247
  806.7 8.1 fusion.118
  814.8 8.2 copy.201
  827.3 6.1 bitcast_convert_fusion.6
  833.5 10.3 bitcast_convert_fusion.1
  843.8 9.3 bitcast_convert_fusion
  857.3 63.0 %all-reduce.6 = (bf16[768]{0:T(1024)(128)(2,1)S(1)}, bf16[3072]{0:T(1024)(128)(2,1)S(1)}, bf16[768]{0:T(1024)(128)(2,1)S(1)}) all-reduce(bf16[768]{0:T(1024)(128)(2,1)S(1)} %dynamic-update-slice.1, bf16[3072]{0:T(1024)(128)(2,1)S(1)} %copy-done.41, bf16[768]{0:T(1024)(128)(2,1)S(1)} %reduce_sum.248), channel_id=1, replica_groups=mesh['mem'=2,'fsdp'=16] {'fsdp'}, use_global_device_ids=true, to_apply=%add.1 | all-reduce | flops 4608 | bytes 18432
  920.3 9.9 bitcast_reduce_fusion
  931.1 3.2 fusion.125
  935.4 73.6 %all-reduce.13.cloned.1.call-done = (bf16[3,768,768]{2,0,1:T(4,128)(2,1)}, bf16[3,768,768]{2,0,1:T(4,128)(2,1)}) async-done(((bf16[3,768,768]{2,0,1:T(4,128)(2,1)}, bf16[3,768,768]{2,0,1:T(4,128)(2,1)}), (bf16[3,768,768]{2,0,1:T(4,128)(2,1)}, bf16[3,768,768]{2,0,1:T(4,128)(2,1)})) %all-reduce.13.cloned.1.call-update) | async-done | bytes 7077904
  1012.5 58.5 %reduce-scatter.25.cloned.1.call-done = bf16[48,768]{1,0:T(8,128)(2,1)} async-done(((bf16[768,768]{1,0:T(8,128)(2,1)}), bf16[48,768]{1,0:T(8,128)(2,1)}) %reduce-scatter.25.cloned.1.call-update) | async-done | bytes 73744 | tf_op jit(solution)/shard_map/reduce_scatter | solution.py:280
  1071.1 61.0 %reduce-scatter.23.cloned.1.call-done = bf16[48,768]{1,0:T(8,128)(2,1)} async-done(((bf16[768,768]{1,0:T(8,128)(2,1)}), bf16[48,768]{1,0:T(8,128)(2,1)}) %reduce-scatter.23.cloned.1.call-update) | async-done | bytes 73744 | tf_op jit(solution)/shard_map/reduce_scatter | solution.py:274
  1132.0 78.8 %reduce-scatter.27.cloned.1.call-done = bf16[48,3072]{1,0:T(8,128)(2,1)} async-done(((bf16[768,3072]{1,0:T(8,128)(2,1)}), bf16[48,3072]{1,0:T(8,128)(2,1)}) %reduce-scatter.27.cloned.1.call-update) | async-done | bytes 294928 | tf_op jit(solution)/shard_map/reduce_scatter | solution.py:283
  1210.9 78.3 %reduce-scatter.29.cloned.1.call-done = bf16[192,768]{1,0:T(8,128)(2,1)} async-done(((bf16[3072,768]{1,0:T(8,128)(2,1)}), bf16[192,768]{1,0:T(8,128)(2,1)}) %reduce-scatter.29.cloned.1.call-update) | async-done | bytes 294928 | tf_op jit(solution)/shard_map/reduce_scatter | solution.py:286
  1289.2 9.9 add_convert_fusion.1
  1304.1 42.1 %reduce-scatter.33.cloned.1.call-done = bf16[48,3]{1,0:T(8,128)(2,1)} async-done(((bf16[768,3]{1,0:T(8,128)(2,1)}), bf16[48,3]{1,0:T(8,128)(2,1)}) %reduce-scatter.33.cloned.1.call-update) | async-done | bytes 304
  1347.0 56.3 %reduce-scatter.31.cloned.1.call-done = bf16[48,3]{1,0:T(8,128)(2,1)} async-done(((bf16[768,3]{1,0:T(8,128)(2,1)}), bf16[48,3]{1,0:T(8,128)(2,1)}) %reduce-scatter.31.cloned.1.call-update) | async-done | bytes 304
  1404.1 4.9 all-reduce.8
  1411.3 41.4 %all-reduce.15.cloned.1.call-done = (bf16[3,48,768]{2,0,1:T(4,128)(2,1)}, bf16[3,48,768]{2,0,1:T(4,128)(2,1)}, bf16[48,768]{1,0:T(8,128)(2,1)}, bf16[48,768]{1,0...) async-done(((bf16[3,48,768]{2,0,1:T(4,128)(2,1)}, bf16[3,48,768]{2,0,1:T(4,128)(2,1)}, bf16[48,768]{1,0:T(8,128)(2,1)}, bf16[48,768]{1,0:T(8,128)(2,1)}, ...) | async-done | bytes 1179664 | tf_op jit(solution)/shard_map/psum | solution.py:303
  (557 shorter events, 411.4 us)
Async XLA Ops:
  7.2 45.3 %copy-start.5 = (bf16[2,512,768]{2,1,0:T(8,128)(2,1)S(1)}, bf16[2,512,768]{2,1,0:T(8,128)(2,1)}, u32[]{:S(2)}) copy-start(bf16[2,512,768]{2,1,0:T(8,128)(2,1)} %param.24) | copy-start | bytes 4718596
  7.2 53.1 %all-gather.13.cloned.1.call-start = ((), (), s32[]{:S(2)}) async-start(), calls=%async_computation.10 | async-start | bytes 3760128 | tf_op jit(solution)/shard_map/all_gather | solution.py:133
  7.9 113.9 %all-gather.17.cloned.1.call-start = ((), (), s32[]{:S(2)}) async-start(), calls=%async_computation.12 | async-start | bytes 3760128 | tf_op jit(solution)/shard_map/all_gather | solution.py:135
  8.7 147.1 %all-gather.25.cloned.1.call-start = ((), (), s32[]{:S(2)}) async-start(), calls=%async_computation.24 | async-start | bytes 4718592 | tf_op jit(solution)/shard_map/all_gather | solution.py:163
  50.7 9.6 copy-start.29
  50.7 9.6 copy-start.44
  50.7 249.1 %copy-start.33 = (f32[768]{0:T(1024)}, f32[768]{0:T(1024)S(1)}, u32[]{:S(2)}) copy-start(f32[768]{0:T(1024)S(1)} %get-tuple-element.649) | copy-start | bytes 9220
  52.4 7.9 copy-start.25
  53.0 7.3 copy-start.31
  53.1 7.3 copy-start.27
  68.7 3.8 copy-start.51
  68.7 3.9 copy-start.21
  68.7 15.8 %copy-start.56 = (s32[2]{0:T(128)S(1)}, s32[2]{0:T(128)}, u32[]{:S(2)}) copy-start(s32[2]{0:T(128)} %param.29) | copy-start | bytes 28
  68.7 15.8 %copy-start.47 = (u32[32]{0:T(128)S(1)}, u32[32]{0:T(128)}, u32[]{:S(2)}) copy-start(u32[32]{0:T(128)} %constant.196) | copy-start | bytes 388
  68.7 17.1 %copy-start.57 = (bf16[192]{0:T(256)(128)(2,1)S(1)}, bf16[192]{0:T(256)(128)(2,1)}, u32[]{:S(2)}) copy-start(bf16[192]{0:T(256)(128)(2,1)} %param.36) | copy-start | bytes 1156
  68.7 134.0 %all-gather.27.cloned.1.call-start = ((), (), s32[]{:S(2)}) async-start(), calls=%async_computation.25 | async-start | bytes 4718592 | tf_op jit(solution)/shard_map/all_gather | solution.py:164
  69.3 225.0 %all-gather.15.cloned.1.call-start = ((), (), s32[]{:S(2)}) async-start(), calls=%async_computation.11 | async-start | bytes 1253376 | tf_op jit(solution)/shard_map/all_gather | solution.py:134
  69.9 281.3 %all-gather.19.cloned.1.call-start = ((), (), s32[]{:S(2)}) async-start(), calls=%async_computation.13 | async-start | bytes 1253376 | tf_op jit(solution)/shard_map/all_gather | solution.py:136
  70.4 286.4 %all-gather.21.cloned.1.call-start = ((), (), s32[]{:S(2)}) async-start(), calls=%async_computation.14 | async-start | bytes 5013504 | tf_op jit(solution)/shard_map/all_gather | solution.py:137
  71.2 333.2 %all-gather.23.cloned.1.call-start = ((), (), s32[]{:S(2)}) async-start(), calls=%async_computation.15 | async-start | bytes 5013504 | tf_op jit(solution)/shard_map/all_gather | solution.py:138
  71.9 659.6 %reduce-scatter.19.cloned.1.call-start = ((), (), s32[]{:S(2)}) async-start(), calls=%async_computation.18 | async-start | bytes 1179648 | tf_op jit(solution)/shard_map/reduce_scatter | solution.py:219
  306.7 4.1 copy-start.58
  356.8 76.9 %copy-start.36 = (f32[2,512]{1,0:T(2,128)}, f32[2,512]{1,0:T(2,128)S(1)}, u32[]{:S(2)}) copy-start(f32[2,512]{1,0:T(2,128)S(1)} %fusion.167) | copy-start | bytes 12292
  404.4 19.4 %copy-start.1 = (f32[2,512,768]{2,1,0:T(8,128)S(1)}, f32[2,512,768]{2,1,0:T(8,128)}, u32[]{:S(2)}) copy-start(f32[2,512,768]{2,1,0:T(8,128)} %copy-done) | copy-start | bytes 9437188
  444.3 100.5 %copy-start.34 = (f32[768]{0:T(1024)S(1)}, f32[768]{0:T(1024)}, u32[]{:S(2)}) copy-start(f32[768]{0:T(1024)} %copy-done.33) | copy-start | bytes 9220
  553.0 178.6 %reduce-scatter.21.cloned.1.call-start = ((), (), s32[]{:S(2)}) async-start(), calls=%async_computation.19 | async-start | bytes 1179648 | tf_op jit(solution)/shard_map/reduce_scatter | solution.py:222
  553.1 3.6 copy-start.4
  553.1 3.6 copy-start.11
  556.7 4.6 copy-start.53
  568.8 192.3 %reduce-scatter.15.cloned.1.call-start = ((), (), s32[]{:S(2)}) async-start(), calls=%async_computation.16 | async-start | bytes 4718592 | tf_op jit(solution)/shard_map/reduce_scatter | solution.py:244
  717.6 89.0 %reduce-scatter.17.cloned.1.call-start = ((), (), s32[]{:S(2)}) async-start(), calls=%async_computation.17 | async-start | bytes 4718592 | tf_op jit(solution)/shard_map/reduce_scatter | solution.py:247
  722.4 3.3 copy-start.35
  722.4 286.6 %all-reduce.13.cloned.1.call-start = ((), (), s32[]{:S(2)}) async-start(), calls=%async_computation.28 | async-start | bytes 18874368
  725.7 6.0 copy-start.22
  735.6 71.0 %copy-start.6 = (bf16[2,512,768]{2,1,0:T(8,128)(2,1)S(1)}, bf16[2,512,768]{2,1,0:T(8,128)(2,1)}, u32[]{:S(2)}) copy-start(bf16[2,512,768]{2,1,0:T(8,128)(2,1)} %param.24) | copy-start | bytes 4718596
  735.6 71.0 %copy-start.17 = (bf16[1,2,512,768]{3,2,0,1:T(8,128)(2,1)S(1)}, bf16[1,2,512,768]{3,2,0,1:T(8,128)(2,1)}, u32[]{:S(2)}) copy-start(bf16[1,2,512,768]{3,2,0,1:T(8,128)(2,1)} %copy.195) | copy-start | bytes 4718596
  735.6 71.0 %copy-start.26 = (f32[2,512]{1,0:T(2,128)S(1)}, f32[2,512]{1,0:T(2,128)}, u32[]{:S(2)}) copy-start(f32[2,512]{1,0:T(2,128)} %copy-done.25) | copy-start | bytes 12292
  735.6 71.0 %copy-start.28 = (f32[2,512]{1,0:T(2,128)S(1)}, f32[2,512]{1,0:T(2,128)}, u32[]{:S(2)}) copy-start(f32[2,512]{1,0:T(2,128)} %copy-done.27) | copy-start | bytes 12292
  735.7 71.0 %copy-start.30 = (f32[768]{0:T(1024)S(1)}, f32[768]{0:T(1024)}, u32[]{:S(2)}) copy-start(f32[768]{0:T(1024)} %copy-done.29) | copy-start | bytes 9220
  735.7 71.0 %copy-start.45 = (f32[768]{0:T(1024)S(1)}, f32[768]{0:T(1024)}, u32[]{:S(2)}) copy-start(f32[768]{0:T(1024)} %copy-done.44) | copy-start | bytes 9220
  822.9 248.1 %reduce-scatter.25.cloned.1.call-start = ((), (), s32[]{:S(2)}) async-start(), calls=%async_computation.21 | async-start | bytes 1253376 | tf_op jit(solution)/shard_map/reduce_scatter | solution.py:280
  827.2 6.2 copy-start.2
  827.2 6.2 copy-start.37
  827.3 6.2 copy-start.39
  827.3 6.2 copy-start.43
  827.3 304.8 %reduce-scatter.23.cloned.1.call-start = ((), (), s32[]{:S(2)}) async-start(), calls=%async_computation.20 | async-start | bytes 1253376 | tf_op jit(solution)/shard_map/reduce_scatter | solution.py:274
  833.4 377.4 %reduce-scatter.27.cloned.1.call-start = ((), (), s32[]{:S(2)}) async-start(), calls=%async_computation.22 | async-start | bytes 5013504 | tf_op jit(solution)/shard_map/reduce_scatter | solution.py:283
  843.8 445.4 %reduce-scatter.29.cloned.1.call-start = ((), (), s32[]{:S(2)}) async-start(), calls=%async_computation.23 | async-start | bytes 5013504 | tf_op jit(solution)/shard_map/reduce_scatter | solution.py:286
  853.2 3.8 copy-start.59
  853.2 4.0 copy-start.50
  853.2 4.0 copy-start.49
  853.2 4.1 copy-start.40
  853.2 4.1 copy-start.48
  853.2 4.1 copy-start.41
  853.2 492.9 %reduce-scatter.33.cloned.1.call-start = ((), (), s32[]{:S(2)}) async-start(), calls=%async_computation.27 | async-start | bytes 208896
  920.3 10.8 copy-start.32
  934.4 468.9 %reduce-scatter.31.cloned.1.call-start = ((), (), s32[]{:S(2)}) async-start(), calls=%async_computation.26 | async-start | bytes 208896
  935.3 517.3 %all-reduce.15.cloned.1.call-start = ((), (), s32[]{:S(2)}) async-start(), calls=%async_computation.29 | async-start | bytes 2654208 | tf_op jit(solution)/shard_map/psum | solution.py:303
  1289.2 10.1 copy-start.52
  1289.2 10.0 copy-start.54
  1289.2 10.0 copy-start.55
  1289.2 11.8 copy-start.14
  1452.6 7.2 copy-start.24
  1452.6 7.9 copy-start.23
  (27 other events, 47.2 us)
Sparse Core Ops, SparseCore 0:
  10.3 49.9 all-gather.12
  62.6 47.0 all-gather.16
  111.8 43.9 all-gather.24
  157.8 44.9 all-gather.26
  204.9 38.5 all-gather.14
  245.6 37.3 all-gather.18
  285.2 52.2 all-gather.20
  339.9 52.0 all-gather.22
  553.1 17.3 reduce-scatter.18
  573.3 17.4 reduce-scatter.20
  717.8 43.3 reduce-scatter.14
  763.3 43.3 reduce-scatter.16
  823.1 185.8 all-reduce.12
  1012.9 58.1 reduce-scatter.24
  1075.0 57.0 reduce-scatter.22
  1136.3 74.5 reduce-scatter.26
  1214.6 74.5 reduce-scatter.28
  1293.5 52.6 reduce-scatter.32
  1350.6 52.6 reduce-scatter.30
  1406.5 46.0 all-reduce.14
where the time goes:
time: 1480 us; the launch traced here: 1470 us
  waiting for transfers between devices  632 us (43%)
  matrix products  475 us (32%)
  blocking collectives  153 us (10%)
  local copies, waits for them, and re-layouts  98 us (7%)
  other arithmetic  89.4 us (6%)
  between operations  18.2 us (1%)
    unnamed x23, waiting for transfers between devices  177 us
    unnamed x2, blocking collectives  95.4 us
    dot_general x48, matrix products, head_scores(): jnp.einsum('cti,cvi->ctv', query_matrix, key_matrix, preferred_element_ty...  94 us
    reduce_scatter x1, waiting for transfers between devices, body(): lax.psum_scatter(full_grads[4].astype(jnp.bfloat16), 'fsdp', scatter_dime...  78.8 us
    reduce_scatter x1, waiting for transfers between devices, body(): lax.psum_scatter(full_grads[5].astype(jnp.bfloat16), 'fsdp', scatter_dime...  78.3 us
    dot_general x24, matrix products, one_head(): jnp.einsum('zqf,zfm->zqm', reduced_probabilities, head_value_rows, prefer...  61 us
    reduce_scatter x1, waiting for transfers between devices, body(): lax.psum_scatter(full_grads[1].astype(jnp.bfloat16), 'fsdp', scatter_dime...  61 us
    reduce_scatter x1, waiting for transfers between devices, body(): lax.psum_scatter(full_grads[3].astype(jnp.bfloat16), 'fsdp', scatter_dime...  58.5 us
  transfers between devices with their start and end apart: 20, of which 13 were waited for; matrix products, arithmetic and copies ran while one was open for 33% of the time, Pallas kernels for 0%

commit v1 on v0

--- a/solution.py
+++ b/solution.py
@@ -1,12 +1,396 @@
 import jax
 import jax.numpy as jnp
 from jax import lax
+from jax.experimental import pallas as pl
+from jax.experimental.pallas import tpu as pltpu
 from jax.sharding import PartitionSpec as P
 
-HEAD_FEATURES = 64
-
-
+F32 = jnp.float32
+B16 = jnp.bfloat16
+HEAD = 64
+GROUP = 256
+PER = GROUP // HEAD
 EPSILON = 1e-05
+NEG = -1000000000.0
+
+
+def dot(a, b):
+    return jnp.dot(a, b, preferred_element_type=F32)
+
+
+def dot_nt(a, b):
+    return lax.dot_general(a, b, (((1,), (1,)), ((), ())), preferred_element_type=F32)
+
+
+def dot_tn(a, b):
+    return lax.dot_general(a, b, (((0,), (0,)), ((), ())), preferred_element_type=F32)
+
+
+def norm_parts(v):
+    centre = v - jnp.mean(v, -1, keepdims=True)
+    rs = lax.rsqrt(jnp.mean(centre * centre, -1, keepdims=True) + EPSILON)
+    return centre * rs, rs
+
+
+def norm_back(e, v, gain):
+    n, rs = norm_parts(v)
+    t = e * gain
+    dx = rs * (t - jnp.mean(t, -1, keepdims=True) - n * jnp.mean(t * n, -1, keepdims=True))
+    return dx, jnp.sum(e * n, 0, keepdims=True), jnp.sum(e, 0, keepdims=True)
+
+
+def cols(g):
+    return pl.ds(pl.multiple_of(g * GROUP, GROUP), GROUP)
+
+
+def head_rows(h, rows, width):
+    return lax.broadcasted_iota(jnp.int32, (rows, width), 0) // HEAD == h
+
+
+def head_cols(h, rows, width):
+    return lax.broadcasted_iota(jnp.int32, (rows, width), 1) // HEAD == h
+
+
+def allowed_block(first_key, nk, first_query, nq, limit, causal):
+    key = first_key + lax.broadcasted_iota(jnp.int32, (nk, nq), 0)
+    ok = key < limit
+    if causal:
+        query = first_query + lax.broadcasted_iota(jnp.int32, (nk, nq), 1)
+        ok = ok & (key <= query)
+    return ok
+
+
+def masked_scores(k_ref, kidx, qm, nk, q0, tq, limit, causal):
+    s = dot(k_ref[kidx + (pl.ds(0, nk),)], qm)
+    if causal and nk > tq:
+        top = jnp.where(allowed_block(0, nk - tq, q0, tq, limit, False), s[: nk - tq], NEG)
+        bottom = jnp.where(allowed_block(nk - tq, tq, q0, tq, limit, True), s[nk - tq :], NEG)
+        return jnp.concatenate([top, bottom], 0)
+    return jnp.where(allowed_block(nk - (tq if causal else nk), nk, q0, tq, limit, causal), s, NEG)
+
+
+def attend_group(q_ref, k_ref, v_ref, qi_, ki_, vi_, out_ref, g, lse_ref, limit, causal, tq, qt, vt, ot):
+    L = qt.shape[1]
+    K = vt.shape[1]
+    qt[...] = (q_ref[qi_].astype(F32) * HEAD**-0.5).T.astype(B16)
+    vt[...] = v_ref[vi_].astype(F32).T.astype(B16)
+    for i in range(L // tq):
+        nk = (i + 1) * tq if causal else K
+        for h in range(PER):
+            block = qt[:, i * tq : (i + 1) * tq]
+            qm = jnp.where(head_rows(h, GROUP, tq), block, jnp.zeros_like(block))
+            s = masked_scores(k_ref, ki_, qm, nk, i * tq, tq, limit, causal)
+            m = jnp.max(s, 0, keepdims=True)
+            e = jnp.exp(s - m)
+            total = jnp.sum(e, 0, keepdims=True)
+            p = (e * (1.0 / total)).astype(B16)
+            lse_ref[g, h : h + 1, i * tq : (i + 1) * tq] = m + jnp.log(total)
+            o = dot(vt[h * HEAD : (h + 1) * HEAD, 0:nk], p)
+            ot[h * HEAD : (h + 1) * HEAD, i * tq : (i + 1) * tq] = o.astype(B16)
+    out_ref[:, cols(g)] = ot[...].astype(F32).T.astype(B16)
+
+
+def attend_back_group(
+    q_ref, k_ref, v_ref, qi_, ki_, vi_, a_ref, da_ref, g, lse_ref, limit, causal, tq,
+    qt, kt, at, dat, ps, dss, qm_ref, dm_ref, dqt, dk_acc, dv_acc,
+):
+    L = qt.shape[1]
+    K = kt.shape[1]
+    scale = HEAD**-0.5
+    qt[...] = (q_ref[qi_].astype(F32) * scale).T.astype(B16)
+    kt[...] = (k_ref[ki_].astype(F32) * scale).T.astype(B16)
+    at[...] = a_ref[:, cols(g)].astype(F32).T
+    dat[...] = da_ref[:, cols(g)].astype(F32).T.astype(B16)
+    if causal:
+        dk_acc[...] = jnp.zeros_like(dk_acc)
+        dv_acc[...] = jnp.zeros_like(dv_acc)
+    for i in range(L // tq):
+        nk = (i + 1) * tq if causal else K
+        span = slice(i * tq, (i + 1) * tq)
+        qn = q_ref[qi_ + (pl.ds(i * tq, tq),)] * jnp.asarray(scale, B16)
+        dn = da_ref[pl.ds(i * tq, tq), cols(g)]
+        for h in range(PER):
+            hs = slice(h * HEAD, (h + 1) * HEAD)
+            here = head_rows(h, GROUP, tq)
+            block = qt[:, span]
+            qm = jnp.where(here, block, jnp.zeros_like(block))
+            block = dat[:, span]
+            dm = jnp.where(here, block, jnp.zeros_like(block))
+            delta = jnp.sum(at[hs, span] * dat[hs, span].astype(F32), 0, keepdims=True)
+            s = masked_scores(k_ref, ki_, qm, nk, i * tq, tq, limit, causal)
+            p = jnp.exp(s - lse_ref[g, h : h + 1, span])
+            dp = dot(v_ref[vi_ + (pl.ds(0, nk),)], dm)
+            ds = (p * (dp - delta)).astype(B16)
+            ps[0:nk, h * tq : (h + 1) * tq] = p.astype(B16)
+            dss[0:nk, h * tq : (h + 1) * tq] = ds
+            dqt[hs, span] = dot(kt[hs, 0:nk], ds)
+            mine = head_cols(h, tq, GROUP)
+            qm_ref[h * tq : (h + 1) * tq] = jnp.where(mine, qn, jnp.zeros_like(qn))
+            dm_ref[h * tq : (h + 1) * tq] = jnp.where(mine, dn, jnp.zeros_like(dn))
+        dvi = dot(ps[0:nk], dm_ref[...])
+        dki = dot(dss[0:nk], qm_ref[...])
+        if causal:
+            dv_acc[0:nk] += dvi
+            dk_acc[0:nk] += dki
+        elif i == 0:
+            dv_acc[...] = dvi
+            dk_acc[...] = dki
+        else:
+            dv_acc[...] += dvi
+            dk_acc[...] += dki
+
+
+ERFCX = (
+    0.21161358920977177, 0.2106475215974073, 0.20533035663075158, 0.12143152976148842,
+    0.27391662866419597, -0.22972237163936396, 0.432698311257476, -0.287490481514182,
+    0.06157492612604076,
+)
+
+
+def gelu_parts(u):
+    z = jnp.abs(u) * 0.7071067811865476
+    t = 1.0 / (1.0 + 0.375 * z)
+    poly = jnp.full_like(t, ERFCX[8])
+    for c in ERFCX[7::-1]:
+        poly = poly * t + c
+    bell = jnp.exp(-0.5 * u * u)
+    half = 0.5 * (poly * t) * bell
+    cdf = jnp.where(u >= 0, 1.0 - half, half)
+    return u * cdf, cdf + u * (bell * 0.3989422804014327)
+
+
+ROWS = 256
+
+
+def self_forward(tlen, tokens, gains, shifts, w, proj, h1, qkv, a, lse, x1, qt, vt, ot):
+    L, D = tokens.shape
+    for r in range(0, L, ROWS):
+        rs = pl.ds(r, ROWS)
+        n, _ = norm_parts(tokens[rs].astype(F32))
+        h1[rs] = (n * gains[0:1] + shifts[0:1]).astype(B16)
+
+    def group(g, _):
+        for k in range(3):
+            qkv[k, g] = dot(h1[...], w[k, :, cols(g)]).astype(B16)
+        attend_group(qkv, qkv, qkv, (0, g), (1, g), (2, g), a, g, lse, tlen[0], True, 256, qt, vt, ot)
+        return 0
+
+    lax.fori_loop(0, D // GROUP, group, 0)
+    for r in range(0, L, ROWS):
+        rs = pl.ds(r, ROWS)
+        x1[rs] = tokens[rs].astype(F32) + dot(a[rs], proj[...])
+
+
+def cross_forward(mlen, flag, x1, mem, gains, shifts, w, proj, h2, cq, ckv, c, lse, x2, qt, vt, ot):
+    L, D = x1.shape
+    for r in range(0, L, ROWS):
+        rs = pl.ds(r, ROWS)
+        n, _ = norm_parts(x1[rs])
+        h2[rs] = (n * gains[1:2] + shifts[1:2]).astype(B16)
+
+    def group(g, _):
+        cq[g] = dot(h2[...], w[0, :, cols(g)]).astype(B16)
+        ckv[0, g] = dot(mem[...], w[1, :, cols(g)]).astype(B16)
+        ckv[1, g] = dot(mem[...], w[2, :, cols(g)]).astype(B16)
+        attend_group(cq, ckv, ckv, (g,), (0, g), (1, g), c, g, lse, mlen[0], False, 256, qt, vt, ot)
+        return 0
+
+    lax.fori_loop(0, D // GROUP, group, 0)
+    f = flag[0].astype(F32)
+    for r in range(0, L, ROWS):
+        rs = pl.ds(r, ROWS)
+        x2[rs] = x1[rs] + f * dot(c[rs], proj[...])
+
+
+def feed_forward(x2, cot, gains, shifts, w_in, w_out, b_in, b_out, mixed, g2, gw_in, gw_out, gb_in, vecs,
+                 h3, h3t, acc, dh3, act, dpre, tf=512):
+    L, D = x2.shape
+    FF = w_in.shape[1]
+    gb_out = jnp.zeros((1, D), F32)
+    for r in range(0, L, ROWS):
+        rs = pl.ds(r, ROWS)
+        n, _ = norm_parts(x2[rs])
+        h = n * gains[2:3] + shifts[2:3]
+        h3[rs] = h.astype(B16)
+        h3t[:, r : r + ROWS] = h.T.astype(B16)
+        acc[rs] = x2[rs] + b_out[...]
+        dh3[rs] = jnp.zeros((ROWS, D), F32)
+        gb_out += jnp.sum(cot[rs].astype(F32), 0, keepdims=True)
+    vecs[2:3] = gb_out
+
+    def tile(f, _):
+        fs = pl.ds(pl.multiple_of(f * tf, tf), tf)
+        gb = jnp.zeros((1, tf), F32)
+        for r in range(0, L, ROWS):
+            rs = pl.ds(r, ROWS)
+            pre = dot(h3[rs], w_in[:, fs]) + b_in[:, fs]
+            up, slope = gelu_parts(pre)
+            act[rs] = up.astype(B16)
+            acc[rs] += dot(act[rs], w_out[fs])
+            d = (dot_nt(cot[rs], w_out[fs]) * slope).astype(B16)
+            dpre[rs] = d
+            gb += jnp.sum(d.astype(F32), 0, keepdims=True)
+            dh3[rs] += dot_nt(d, w_in[:, fs])
+        gb_in[:, fs] = gb
+        gw_out[fs] = dot_tn(act[...], cot[...]).astype(B16)
+        gw_in[:, fs] = dot(h3t[...], dpre[...]).astype(B16)
+        return 0
+
+    lax.fori_loop(0, FF // tf, tile, 0)
+    sg = jnp.zeros((1, D), F32)
+    sb = jnp.zeros((1, D), F32)
+    for r in range(0, L, ROWS):
+        rs = pl.ds(r, ROWS)
+        mixed[rs] = acc[rs].astype(B16)
+        dx, a, b = norm_back(dh3[rs], x2[rs], gains[2:3])
+        g2[rs] = cot[rs].astype(F32) + dx
+        sg += a
+        sb += b
+    vecs[0:1] = sg
+    vecs[1:2] = sb
+
+
+def cross_backward(mlen, flag, g2, x1, mem, gains, w, proj, h2, cq, ckv, c, lse,
+                   g1, gmem, gw, gproj, vecs,
+                   gc, dc, dcq, dck, dcv, dh2, qt, kt, at, dat, ps, dss, qm, dm, dqt, dk_acc, dv_acc):
+    L, D = x1.shape
+    f = flag[0].astype(F32)
+    for r in range(0, L, ROWS):
+        rs = pl.ds(r, ROWS)
+        gcr = (f * g2[rs]).astype(B16)
+        gc[rs] = gcr
+        dc[rs] = dot_nt(gcr, proj[...]).astype(B16)
+        dh2[rs] = jnp.zeros((ROWS, D), F32)
+    gmem[...] = jnp.zeros_like(gmem)
+
+    def gproj_tile(t, _):
+        gproj[cols(t)] = dot_tn(c[:, cols(t)], gc[...]).astype(B16)
+        return 0
+
+    lax.fori_loop(0, D // GROUP, gproj_tile, 0)
+
+    def group(g, _):
+        attend_back_group(cq, ckv, ckv, (g,), (0, g), (1, g), c, dc, g, lse, mlen[0], False, 256,
+                          qt, kt, at, dat, ps, dss, qm, dm, dqt, dk_acc, dv_acc)
+        dcq[...] = dqt[...].T.astype(B16)
+        dck[...] = dk_acc[...].astype(B16)
+        dcv[...] = dv_acc[...].astype(B16)
+        gw[0, :, cols(g)] = dot_tn(h2[...], dcq[...]).astype(B16)
+        gw[1, :, cols(g)] = dot_tn(mem[...], dck[...]).astype(B16)
+        gw[2, :, cols(g)] = dot_tn(mem[...], dcv[...]).astype(B16)
+        dh2[...] += dot_nt(dcq[...], w[0, :, cols(g)])
+        gmem[...] += dot_nt(dck[...], w[1, :, cols(g)]) + dot_nt(dcv[...], w[2, :, cols(g)])
+        return 0
+
+    lax.fori_loop(0, D // GROUP, group, 0)
+    sg = jnp.zeros((1, D), F32)
+    sb = jnp.zeros((1, D), F32)
+    for r in range(0, L, ROWS):
+        rs = pl.ds(r, ROWS)
+        dx, a, b = norm_back(dh2[rs], x1[rs], gains[1:2])
+        g1[rs] = g2[rs] + dx
+        sg += a
+        sb += b
+    vecs[0:1] = sg
+    vecs[1:2] = sb
+
+
+def self_backward(tlen, g1, tokens, gains, w, proj, h1, qkv, a, lse,
+                  gtok, gw, gproj, vecs,
+                  ga, da, dq, dk, dv, dh1, qt, kt, at, dat, ps, dss, qm, dm, dqt, dk_acc, dv_acc):
+    L, D = tokens.shape
+    for r in range(0, L, ROWS):
+        rs = pl.ds(r, ROWS)
+        gar = g1[rs].astype(B16)
+        ga[rs] = gar
+        da[rs] = dot_nt(gar, proj[...]).astype(B16)
+        dh1[rs] = jnp.zeros((ROWS, D), F32)
+
+    def gproj_tile(t, _):
+        gproj[cols(t)] = dot_tn(a[:, cols(t)], ga[...]).astype(B16)
+        return 0
+
+    lax.fori_loop(0, D // GROUP, gproj_tile, 0)
+
+    def group(g, _):
+        attend_back_group(qkv, qkv, qkv, (0, g), (1, g), (2, g), a, da, g, lse, tlen[0], True, 256,
+                          qt, kt, at, dat, ps, dss, qm, dm, dqt, dk_acc, dv_acc)
+        dq[...] = dqt[...].T.astype(B16)
+        dk[...] = dk_acc[...].astype(B16)
+        dv[...] = dv_acc[...].astype(B16)
+        for k, d in enumerate((dq, dk, dv)):
+            gw[k, :, cols(g)] = dot_tn(h1[...], d[...]).astype(B16)
+            dh1[...] += dot_nt(d[...], w[k, :, cols(g)])
+        return 0
+
+    lax.fori_loop(0, D // GROUP, group, 0)
+    sg = jnp.zeros((1, D), F32)
+    sb = jnp.zeros((1, D), F32)
+    for r in range(0, L, ROWS):
+        rs = pl.ds(r, ROWS)
+        dx, x, b = norm_back(dh1[rs], tokens[rs].astype(F32), gains[0:1])
+        gtok[rs] = (g1[rs] + dx).astype(gtok.dtype)
+        sg += x
+        sb += b
+    vecs[0:1] = sg
+    vecs[1:2] = sb
+
+
+VMEM = pltpu.VMEM
+SMEM_SPEC = pl.BlockSpec(memory_space=pltpu.SMEM)
+VMEM_SPEC = pl.BlockSpec(memory_space=pltpu.VMEM)
+
+
+def call(kernel, scalars, arrays, outs, scratch, name):
+    return pl.pallas_call(
+        kernel,
+        out_shape=[jax.ShapeDtypeStruct(s, d) for s, d in outs],
+        in_specs=[SMEM_SPEC] * len(scalars) + [VMEM_SPEC] * len(arrays),
+        out_specs=[VMEM_SPEC] * len(outs),
+        scratch_shapes=[VMEM(s, d) for s, d in scratch],
+        compiler_params=pltpu.CompilerParams(vmem_limit_bytes=60 * 1024 * 1024),
+        name=name,
+    )(*scalars, *arrays)
+
+
+def back_scratch(L, K):
+    return [
+        ((GROUP, L), B16), ((GROUP, K), B16), ((GROUP, L), F32), ((GROUP, L), B16),
+        ((K, PER * 256), B16), ((K, PER * 256), B16), ((PER * 256, GROUP), B16), ((PER * 256, GROUP), B16),
+        ((GROUP, L), F32), ((K, GROUP), F32), ((K, GROUP), F32),
+    ]
+
+
+def layer(tokens, memory, cot, tlen, mlen, flag, self_w, self_proj, cross_w, cross_proj, w_in, w_out, b_in, b_out, gains, shifts):
+    L, D = tokens.shape
+    M = memory.shape[0]
+    FF = w_in.shape[1]
+    G = D // GROUP
+    h1, qkv, a, lse, x1 = call(
+        self_forward, (tlen,), (tokens, gains, shifts, self_w, self_proj),
+        [((L, D), B16), ((3, G, L, GROUP), B16), ((L, D), B16), ((G, 8, L), F32), ((L, D), F32)],
+        [((GROUP, L), B16)] * 3, "self_forward")
+    h2, cq, ckv, c, clse, x2 = call(
+        cross_forward, (mlen, flag), (x1, memory, gains, shifts, cross_w, cross_proj),
+        [((L, D), B16), ((G, L, GROUP), B16), ((2, G, M, GROUP), B16), ((L, D), B16), ((G, 8, L), F32), ((L, D), F32)],
+        [((GROUP, L), B16), ((GROUP, M), B16), ((GROUP, L), B16)], "cross_forward")
+    mixed, g2, gw_in, gw_out, gb_in, v2 = call(
+        feed_forward, (), (x2, cot, gains, shifts, w_in, w_out, b_in, b_out),
+        [((L, D), B16), ((L, D), F32), ((D, FF), B16), ((FF, D), B16), ((1, FF), F32), ((8, D), F32)],
+        [((L, D), B16), ((D, L), B16), ((L, D), F32), ((L, D), F32), ((L, 512), B16), ((L, 512), B16)], "feed_forward")
+    g1, gmem, gcw, gcproj, v1 = call(
+        cross_backward, (mlen, flag), (g2, x1, memory, gains, cross_w, cross_proj, h2, cq, ckv, c, clse),
+        [((L, D), F32), ((M, D), F32), ((3, D, D), B16), ((D, D), B16), ((8, D), F32)],
+        [((L, D), B16), ((L, D), B16), ((L, GROUP), B16), ((M, GROUP), B16), ((M, GROUP), B16), ((L, D), F32)]
+        + back_scratch(L, M), "cross_backward")
+    gtok, gsw, gsproj, v0 = call(
+        self_backward, (tlen,), (g1, tokens, gains, self_w, self_proj, h1, qkv, a, lse),
+        [((L, D), B16), ((3, D, D), B16), ((D, D), B16), ((8, D), F32)],
+        [((L, D), B16), ((L, D), B16), ((L, GROUP), B16), ((L, GROUP), B16), ((L, GROUP), B16), ((L, D), F32)]
+        + back_scratch(L, L), "self_backward")
+    gain_grads = jnp.concatenate([v0[0:1], v1[0:1], v2[0:1]])
+    shift_grads = jnp.concatenate([v0[1:2], v1[1:2], v2[1:2]])
+    return mixed, gtok, gmem, gsw, gsproj, gcw, gcproj, gw_in, gw_out, gb_in, v2[2], gain_grads, shift_grads
 
 
 def layer_norm(values, gain, shift):
@@ -20,7 +404,7 @@
 
 
 def split_heads(values):
-    return values.reshape(values.shape[0], values.shape[1], -1, HEAD_FEATURES).transpose(2, 0, 1, 3)
+    return values.reshape(values.shape[0], values.shape[1], -1, HEAD).transpose(2, 0, 1, 3)
 
 
 def merge_heads(values):
@@ -30,7 +414,7 @@
 def head_scores(query_matrix, key_matrix, allowed):
     logit_scores = jnp.einsum(
         "cti,cvi->ctv", query_matrix, key_matrix, preferred_element_type=jnp.float32
-    ) * HEAD_FEATURES ** (-0.5)
+    ) * HEAD ** (-0.5)
     return jnp.where(allowed, logit_scores, -1000000000.0)
 
 
@@ -81,10 +465,10 @@
         scores_gradient = (probs * (probs_gradient - delta_sum)).astype(jnp.bfloat16)
         d_query = jnp.einsum(
             "zqf,zfm->zqm", scores_gradient, head_key_rows, preferred_element_type=jnp.float32
-        ) * HEAD_FEATURES ** (-0.5)
+        ) * HEAD ** (-0.5)
         d_keys = jnp.einsum(
             "pum,pug->pmg", scores_gradient, head_query_rows, preferred_element_type=jnp.float32
-        ) * HEAD_FEATURES ** (-0.5)
+        ) * HEAD ** (-0.5)
         values_gradient = jnp.einsum(
             "pum,pug->pmg",
             reduced_probabilities,
@@ -107,7 +491,7 @@
     return (merge_heads(d_query), merge_heads(d_keys), merge_heads(values_gradient))
 
 
-def body(
+def general_body(
     tokens,
     memory,
     cotangent,
@@ -328,6 +712,46 @@
     )
 
 
+def paired_body(tokens, memory, cotangent, text_len, mem_len, image_flag, self_qkv, self_out, cross_qkv, cross_out,
+                w_in, w_out, b_in, b_out, norm_gain, norm_bias):
+    me = lax.axis_index("mem")
+
+    def whole(v):
+        return lax.all_to_all(v, "mem", 0, 1, tiled=True)[0]
+
+    def gather(v, axis=0):
+        return lax.all_gather(v, "fsdp", axis=axis, tiled=True)
+
+    def mine(v):
+        return lax.dynamic_slice(v, (me,), (1,))
+
+    outs = layer(
+        whole(tokens), whole(memory), whole(cotangent), mine(text_len), mine(mem_len), mine(image_flag),
+        gather(self_qkv, 1), gather(self_out), gather(cross_qkv, 1), gather(cross_out), gather(w_in), gather(w_out),
+        gather(b_in).astype(F32)[None], gather(b_out).astype(F32)[None],
+        gather(norm_gain, 1).astype(F32), gather(norm_bias, 1).astype(F32))
+    mixed, gtok, gmem = outs[:3]
+
+    def back(v):
+        return lax.all_to_all(v[None], "mem", 1, 0, tiled=True)
+
+    def scatter(v, axis=0):
+        part = lax.psum_scatter(v.astype(B16), "fsdp", scatter_dimension=axis, tiled=True)
+        return lax.psum(part, "mem").astype(F32)
+
+    gsw, gsp, gcw, gcp, gwi, gwo, gbi, gbo, gg, gs = outs[3:]
+    return (back(mixed), back(gtok).astype(F32), back(gmem.astype(B16)).astype(F32),
+            scatter(gsw, 1), scatter(gsp), scatter(gcw, 1), scatter(gcp), scatter(gwi), scatter(gwo),
+            scatter(gbi[0]), scatter(gbo), scatter(gg, 1), scatter(gs, 1))
+
+
+def body(*args):
+    tokens = args[0]
+    if lax.axis_size("mem") == tokens.shape[0] and tokens.shape[1] % 256 == 0:
+        return paired_body(*args)
+    return general_body(*args)
+
+
 def solution(mesh):
     placed = (
         P("fsdp", "mem", None),

time: 1480 us -> 1040 us (0.70)
  matrix products: 475 us -> 0 us
  Pallas kernels: 0 us -> 205 us
  local copies, waits for them, and re-layouts: 98 us -> 33.1 us
  waiting for transfers between devices: 632 us -> 576 us
  other arithmetic: 89.4 us -> 35.8 us
  starting transfers between devices: 0.81 us -> 17.7 us
    dot_general x189 -> x0, matrix products: 475 us -> none  [the longest x48 94 us: head_scores(): jnp.einsum('cti,cvi->ctv', query_matrix, key_matrix, preferred_element_ty...]
    pallas_call x0 -> x5, Pallas kernels: none -> 205 us  [call(): pl.pallas_call(kernel, out_shape=[jax.ShapeDtypeStruct(s, d) for s, d in...]
    unnamed x23 -> x17, waiting for transfers between devices: 177 us -> 64.2 us
    convert_element_type x39 -> x13, other arithmetic: 47.9 us -> 8.91 us  [the longest x10 8.86 us: scatter(): return lax.psum(part, 'mem').astype(F32)]
    all_to_all x0 -> x2, blocking collectives: none -> 34.6 us  [whole(): return lax.all_to_all(v, 'mem', 0, 1, tiled=True)[0]]
    unnamed x2, blocking collectives: 95.4 us -> 62.3 us
    reduce_scatter x8 -> x6, waiting for transfers between devices: 339 us -> 372 us  [scatter(): lax.psum_scatter(v.astype(B16), 'fsdp', scatter_dimension=axis, tiled=True)]
    reduce_sum x32 -> x0, other arithmetic: 31.9 us -> none  [the longest x24 18.9 us: one_head(): row_sum = jnp.sum(expo, -1, keepdims=True)]
  transfers between devices with their start and end apart: 20 -> 19, of which waited for: 13 -> 13; matrix products, arithmetic and copies ran while one was open for 33% -> 6% of each run, Pallas kernels for 0% -> 6%
where the time goes in v1:
time: 1040 us; the launch traced here: 1030 us
  waiting for transfers between devices  576 us (55%)
  Pallas kernels  205 us (20%)
  blocking collectives  141 us (14%)
  other arithmetic  35.8 us (3%)
  local copies, waits for them, and re-layouts  33.1 us (3%)
  starting transfers between devices  17.7 us (2%)
  between operations  17.1 us (2%)
    reduce_scatter x6, waiting for transfers between devices, scatter(): lax.psum_scatter(v.astype(B16), 'fsdp', scatter_dimension=axis, tiled=True)  372 us
    pallas_call x5, Pallas kernels, call(): pl.pallas_call(kernel, out_shape=[jax.ShapeDtypeStruct(s, d) for s, d in...  205 us
    all_gather x6, waiting for transfers between devices, gather(): return lax.all_gather(v, 'fsdp', axis=axis, tiled=True)  104 us
    unnamed x17, waiting for transfers between devices  64.2 us
    unnamed x2, blocking collectives  62.3 us
    all_gather x2, blocking collectives, gather(): return lax.all_gather(v, 'fsdp', axis=axis, tiled=True)  39.1 us
    all_to_all x2, blocking collectives, whole(): return lax.all_to_all(v, 'mem', 0, 1, tiled=True)[0]  34.6 us
    psum x1, waiting for transfers between devices, scatter(): return lax.psum(part, 'mem').astype(F32)  27.9 us
  transfers between devices with their start and end apart: 19, of which 13 were waited for; matrix products, arithmetic and copies ran while one was open for 6% of the time, Pallas kernels for 6%

profile of v1, /device:TPU:0, one launch (start us, length us, event | category | flops | bytes accessed | tf_op | source)
XLA Modules:
  0.0 1025.0 jit_solution(13856047681089352001)
XLA Ops:
  7.2 0.7 all-gather.11.cloned.1.call-update
  8.0 0.7 all-gather.9.cloned.1.call-update
  8.7 0.7 all-gather.15.cloned.1.call-update
  11.1 12.3 %all_to_all.27 = bf16[2,128,768]{2,1,0:T(8,128)(2,1)} all-to-all(bf16[2,128,768]{2,1,0:T(8,128)(2,1)} %param.17), channel_id=1, replica_groups=mesh['mem'=2,'fsdp'=16] {'mem'}, dimensions={0} | all-to-all | bytes 786432 | tf_op jit(solution)/shard_map/all_to_all | solution.py:720
  23.5 22.2 %all_to_all.28 = bf16[2,512,768]{2,1,0:T(8,128)(2,1)} all-to-all(bf16[2,512,768]{2,1,0:T(8,128)(2,1)S(1)} %copy-done.1), channel_id=1, replica_groups=mesh['mem'=2,'fsdp'=16] {'mem'}, dimensions={0} | all-to-all | bytes 3145728 | tf_op jit(solution)/shard_map/all_to_all | solution.py:720
  45.8 3.8 all-to-all-start.2
  49.7 21.6 %all-gather = bf16[16,48,3]{1,2,0:T(4,128)(2,1)S(1)} all-gather(bf16[1,48,3]{1,2,0:T(4,128)(2,1)S(1)} %bitcast.71), channel_id=1, replica_groups=mesh['mem'=2,'fsdp'=16] {'fsdp'}, dimensions={0}, use_global_device_ids=true | all-gather | bytes 4896 | tf_op jit(solution)/shard_map/all_gather | solution.py:723
  71.3 0.7 reshape.71
  72.0 17.5 %all-gather.1 = bf16[16,48,3]{1,2,0:T(4,128)(2,1)S(1)} all-gather(bf16[1,48,3]{1,2,0:T(4,128)(2,1)S(1)} %bitcast.72), channel_id=1, replica_groups=mesh['mem'=2,'fsdp'=16] {'fsdp'}, dimensions={0}, use_global_device_ids=true | all-gather | bytes 4896 | tf_op jit(solution)/shard_map/all_gather | solution.py:723
  89.5 0.7 reshape.72
  94.3 31.7 %all-reduce.5 = (bf16[3072]{0:T(1024)(128)(2,1)S(1)}, bf16[768]{0:T(1024)(128)(2,1)S(1)}) all-reduce(bf16[3072]{0:T(1024)(128)(2,1)S(1)} %dynamic-update-slice, bf16[768]{0:T(1024)(128)(2,1)S(1)} %dynamic-update-slice.1), channel_id=1, replica_groups=mesh['mem'=2,'fsdp'=16] {'fsdp'}, use_global_device_ids=true, to_apply=%add | all-reduce | flops 3840 | bytes 15360
  126.0 0.6 broadcast_in_dim.26
  126.6 0.6 reshape.54.b_out
  127.2 38.2 %self_forward.1 = (bf16[1024,768]{1,0:T(8,128)(2,1)}, bf16[3,3,1024,256]{3,2,1,0:T(8,128)(2,1)}, bf16[1024,768]{1,0:T(8,128)(2,1)}, f32[3,8,1024]{2,1,0:T(8,128)}, f32[1024,768]{1,0:T(8,128)}) custom-call(s32[1]{0:T(128)} %dynamic_slice.11.tlen, bf16[1024,768]{1,0:T(8,128)(2,1)} %bitcast.42, f32[3,768]{1,0:T(4,128)} %bitcast.60, f32[3,768]{1,0:T(4,128)} %bitcast.65, ...), custom_call_target="tpu_custom_call" | custom-call | tf_op jit(solution)/shard_map/self_forward/pallas_call | solution.py:345
  165.4 22.7 %all-gather.13.cloned.1.call-done.w = bf16[3,768,768]{2,1,0:T(8,128)(2,1)} async-done(((bf16[3,48,768]{2,1,0:T(8,128)(2,1)}), bf16[3,768,768]{2,1,0:T(8,128)(2,1)}) %all-gather.13.cloned.1.call-update) | async-done | bytes 3538960 | tf_op jit(solution)/shard_map/all_gather | solution.py:723
  188.1 27.2 %cross_forward.1 = (bf16[1024,768]{1,0:T(8,128)(2,1)}, bf16[3,1024,256]{2,1,0:T(8,128)(2,1)}, bf16[2,3,256,256]{3,2,1,0:T(8,128)(2,1)}, bf16[1024,768]{1,0:T(8,1...) custom-call(s32[1]{0:T(128)} %dynamic_slice.9.mlen, s32[1]{0:T(128)} %dynamic_slice.10.flag, ...), custom_call_target="tpu_custom_call" | custom-call | tf_op jit(solution)/shard_map/cross_forward/pallas_call | solution.py:345
  215.3 27.4 %all-gather.17.cloned.1.call-done.w_in = bf16[768,3072]{1,0:T(8,128)(2,1)} async-done(((bf16[48,3072]{1,0:T(8,128)(2,1)}), bf16[768,3072]{1,0:T(8,128)(2,1)}) %all-gather.17.cloned.1.call-update) | async-done | bytes 4718608 | tf_op jit(solution)/shard_map/all_gather | solution.py:723
  242.8 54.1 %all-gather.19.cloned.1.call-done.w_out = bf16[3072,768]{1,0:T(8,128)(2,1)} async-done(((bf16[192,768]{1,0:T(8,128)(2,1)}), bf16[3072,768]{1,0:T(8,128)(2,1)}) %all-gather.19.cloned.1.call-update) | async-done | bytes 4718608 | tf_op jit(solution)/shard_map/all_gather | solution.py:723
  296.9 58.5 %feed_forward.1 = (bf16[1024,768]{1,0:T(8,128)(2,1)}, f32[1024,768]{1,0:T(8,128)}, bf16[768,3072]{1,0:T(8,128)(2,1)}, bf16[3072,768]{1,0:T(8,128)(2,1)}, f32[1,3072]{1,0:T(1,128)}, /*index=5*/f32[8,768]{1,0:T(8,128)}) custom-call(f32[1024,768]{1,0:T(8,128)} %get-tuple-element.40.x2, bf16[1024,768]{1,0:T(8,128)(2,1)} %bitcast.48, f32[3,768]{1,0:T(4,128)} %bitcast.62, ...), custom_call_target="tpu_custom_call" | custom-call | tf_op jit(solution)/shard_map/feed_forward/pallas_call | solution.py:345
  355.4 34.4 %cross_backward.1 = (f32[1024,768]{1,0:T(8,128)}, f32[256,768]{1,0:T(8,128)}, bf16[3,768,768]{2,1,0:T(8,128)(2,1)}, bf16[768,768]{1,0:T(8,128)(2,1)}, f32[8,768]{1,0:T(8,128)}) custom-call(s32[1]{0:T(128)} %dynamic_slice.9.mlen, s32[1]{0:T(128)} %dynamic_slice.10.flag, f32[1024,768]{1,0:T(8,128)} %get-tuple-element.42.g2, f32[1024,768]{1,0:T(8,128)} %get-tuple-element.39.x1, ...), custom_call_target="tpu_custom_call" | custom-call | tf_op jit(solution)/shard_map/cross_backward/pallas_call | solution.py:345
  389.7 46.7 %self_backward.1 = (bf16[1024,768]{1,0:T(8,128)(2,1)}, bf16[3,768,768]{2,1,0:T(8,128)(2,1)}, bf16[768,768]{1,0:T(8,128)(2,1)}, f32[8,768]{1,0:T(8,128)}) custom-call(s32[1]{0:T(128)} %dynamic_slice.11.tlen, f32[1024,768]{1,0:T(8,128)} %get-tuple-element.48.g1, bf16[1024,768]{1,0:T(8,128)(2,1)} %bitcast.43, f32[3,768]{1,0:T(4,128)} %bitcast.64, ...), custom_call_target="tpu_custom_call" | custom-call | tf_op jit(solution)/shard_map/self_backward/pallas_call | solution.py:345
  436.5 0.7 reduce-scatter.19.cloned.1.call-update
  437.3 0.7 reduce-scatter.13.cloned.1.call-update
  438.6 0.7 reduce-scatter.21.cloned.1.call-update
  439.9 0.6 copy-done.9
  440.5 3.8 copy.58
  444.9 11.6 %reduce.5 = bf16[1024,768]{1,0:T(8,128)(2,1)} reduce(bf16[1024,1,768]{2,1,0:T(2,128)(2,1)S(1)} %bitcast.44, bf16[]{:T(256)} %broadcast.4), dimensions={1}, to_apply=%bitcast.39.reduce_sub_computation | reduce | bytes 3145730
  456.4 2.5 reshape.83
  459.0 0.6 copy.60
  459.6 3.0 reduce.6
  462.6 0.8 reshape.85
  463.5 3.5 all-to-all-start.5
  467.0 7.2 all-to-all-done.5
  474.2 4.6 all-to-all-start.4
  479.0 0.8 copy.46
  479.9 0.8 copy.48
  480.8 12.4 %reduce-scatter.15.cloned.1.call-done = bf16[48,768]{1,0:T(8,128)(2,1)} async-done(((bf16[768,768]{1,0:T(8,128)(2,1)}), bf16[48,768]{1,0:T(8,128)(2,1)}) %reduce-scatter.15.cloned.1.call-update) | async-done | bytes 73744 | tf_op jit(solution)/shard_map/reduce_scatter | solution.py:739
  493.3 60.7 %reduce-scatter.19.cloned.1.call-done = bf16[48,768]{1,0:T(8,128)(2,1)} async-done(((bf16[768,768]{1,0:T(8,128)(2,1)}), bf16[48,768]{1,0:T(8,128)(2,1)}) %reduce-scatter.19.cloned.1.call-update) | async-done | bytes 73744 | tf_op jit(solution)/shard_map/reduce_scatter | solution.py:739
  554.0 70.9 %reduce-scatter.13.cloned.1.call-done = bf16[3,48,768]{2,1,0:T(8,128)(2,1)} async-done(((bf16[3,768,768]{2,1,0:T(8,128)(2,1)}), bf16[3,48,768]{2,1,0:T(8,128)(2,1)}) %reduce-scatter.13.cloned.1.call-update) | async-done | bytes 221200 | tf_op jit(solution)/shard_map/reduce_scatter | solution.py:739
  624.9 70.7 %reduce-scatter.17.cloned.1.call-done = bf16[3,48,768]{2,1,0:T(8,128)(2,1)} async-done(((bf16[3,768,768]{2,1,0:T(8,128)(2,1)}), bf16[3,48,768]{2,1,0:T(8,128)(2,1)}) %reduce-scatter.17.cloned.1.call-update) | async-done | bytes 221200 | tf_op jit(solution)/shard_map/reduce_scatter | solution.py:739
  695.6 78.4 %reduce-scatter.21.cloned.1.call-done = bf16[48,3072]{1,0:T(8,128)(2,1)} async-done(((bf16[768,3072]{1,0:T(8,128)(2,1)}), bf16[48,3072]{1,0:T(8,128)(2,1)}) %reduce-scatter.21.cloned.1.call-update) | async-done | bytes 294928 | tf_op jit(solution)/shard_map/reduce_scatter | solution.py:739
  774.0 78.9 %reduce-scatter.23.cloned.1.call-done = bf16[192,768]{1,0:T(8,128)(2,1)} async-done(((bf16[3072,768]{1,0:T(8,128)(2,1)}), bf16[192,768]{1,0:T(8,128)(2,1)}) %reduce-scatter.23.cloned.1.call-update) | async-done | bytes 294928 | tf_op jit(solution)/shard_map/reduce_scatter | solution.py:739
  852.9 3.8 copy.59
  856.7 11.6 %reduce.4 = bf16[1024,768]{1,0:T(8,128)(2,1)} reduce(bf16[1024,1,768]{2,1,0:T(2,128)(2,1)S(1)} %bitcast.45, bf16[]{:T(256)} %broadcast.4), dimensions={1}, to_apply=%bitcast.40.reduce_sub_computation | reduce | bytes 3145730
  868.3 2.5 reshape.81
  870.8 4.7 all-to-all-start.3
  876.9 30.6 %all-reduce.4 = (bf16[3072]{0:T(1024)(128)(2,1)S(1)}, bf16[768]{0:T(1024)(128)(2,1)S(1)}) all-reduce(bf16[3072]{0:T(1024)(128)(2,1)S(1)} %convert_reduce_fusion, bf16[768]{0:T(1024)(128)(2,1)S(1)} %get-tuple-element.85), channel_id=8, replica_groups=mesh['mem'=2,'fsdp'=16] {'fsdp'}, use_global_device_ids=true, to_apply=%region_12.0.clone | all-reduce | flops 3840 | bytes 15360
  907.7 2.0 reduce-scatter.25.cloned.1.call-done
  909.7 0.8 copy.47
  910.5 55.8 %reduce-scatter.27.cloned.1.call-done = bf16[48,3]{1,0:T(8,128)(2,1)} async-done(((bf16[768,3]{1,0:T(8,128)(2,1)}), bf16[48,3]{1,0:T(8,128)(2,1)}) %reduce-scatter.27.cloned.1.call-update) | async-done | bytes 304
  966.2 0.8 copy.49
  967.0 4.9 all-reduce.6
  974.6 0.9 copy.52
  975.5 2.5 reshape.84
  978.0 1.9 copy.51
  979.9 2.5 reshape.82
  982.4 1.4 copy.50
  983.7 27.9 %all-reduce.10.cloned.1.call-done = (bf16[3,48,768]{2,1,0:T(8,128)(2,1)}, bf16[48,768]{1,0:T(8,128)(2,1)}, bf16[3,48,768]{2,1,0:T(8,128)(2,1)}, bf16[48,768]{1,0...) async-done(((bf16[3,48,768]{2,1,0:T(8,128)(2,1)}, bf16[48,768]{1,0:T(8,128)(2,1)}, bf16[3,48,768]{2,1,0:T(8,128)(2,1)}, bf16[48,768]{1,0:T(8,128)(2,1)}, ...) | async-done | bytes 1179664 | tf_op jit(solution)/shard_map/psum | solution.py:740
  1011.6 1.9 convert_element_type.76
  1013.5 1.8 convert_element_type.77
  1015.3 0.8 convert_element_type.72
  1016.1 0.8 convert_element_type.74
  1016.9 0.7 convert_element_type.73
  1017.6 0.7 convert_element_type.75
  (94 shorter events, 9.7 us)
Async XLA Ops:
  7.2 16.3 %copy-start.1 = (bf16[2,512,768]{2,1,0:T(8,128)(2,1)S(1)}, bf16[2,512,768]{2,1,0:T(8,128)(2,1)}, u32[]{:S(2)}) copy-start(bf16[2,512,768]{2,1,0:T(8,128)(2,1)} %param.16) | copy-start | bytes 4718596
  7.2 120.0 %all-gather.11.cloned.1.call-start = ((), (), s32[]{:S(2)}) async-start(), calls=%async_computation.15 | async-start | bytes 1253376 | tf_op jit(solution)/shard_map/all_gather | solution.py:723
  7.9 119.3 %all-gather.9.cloned.1.call-start = ((), (), s32[]{:S(2)}) async-start(), calls=%async_computation.14 | async-start | bytes 3760128 | tf_op jit(solution)/shard_map/all_gather | solution.py:723
  8.7 156.7 %all-gather.15.cloned.1.call-start = ((), (), s32[]{:S(2)}) async-start(), calls=%async_computation.17 | async-start | bytes 1253376 | tf_op jit(solution)/shard_map/all_gather | solution.py:723
  9.4 178.7 %all-gather.13.cloned.1.call-start = ((), (), s32[]{:S(2)}) async-start(), calls=%async_computation.16 | async-start | bytes 3760128 | tf_op jit(solution)/shard_map/all_gather | solution.py:723
  10.0 232.8 %all-gather.17.cloned.1.call-start = ((), (), s32[]{:S(2)}) async-start(), calls=%async_computation.18 | async-start | bytes 5013504 | tf_op jit(solution)/shard_map/all_gather | solution.py:723
  10.6 286.3 %all-gather.19.cloned.1.call-start = ((), (), s32[]{:S(2)}) async-start(), calls=%async_computation.19 | async-start | bytes 5013504 | tf_op jit(solution)/shard_map/all_gather | solution.py:723
  45.7 4.0 copy-start.12
  45.7 26.3 %copy-start.13 = (bf16[3,48]{1,0:T(4,128)(2,1)S(1)}, bf16[3,48]{1,0:T(4,128)(2,1)}, u32[]{:S(2)}) copy-start(bf16[3,48]{1,0:T(4,128)(2,1)} %param.31) | copy-start | bytes 868
  45.7 44.5 %copy-start.14 = (s32[2]{0:T(128)S(1)}, s32[2]{0:T(128)}, u32[]{:S(2)}) copy-start(s32[2]{0:T(128)} %param.19) | copy-start | bytes 28
  45.7 45.1 %copy-start.15 = (s32[2]{0:T(128)S(1)}, s32[2]{0:T(128)}, u32[]{:S(2)}) copy-start(s32[2]{0:T(128)} %param.21) | copy-start | bytes 28
  45.7 45.6 %copy-start.16 = (s32[2]{0:T(128)S(1)}, s32[2]{0:T(128)}, u32[]{:S(2)}) copy-start(s32[2]{0:T(128)} %param.20) | copy-start | bytes 28
  45.7 46.2 %copy-start.11 = (u32[32]{0:T(128)S(1)}, u32[32]{0:T(128)}, u32[]{:S(2)}) copy-start(u32[32]{0:T(128)} %constant.18) | copy-start | bytes 388
  45.7 48.1 %copy-start.17 = (bf16[192]{0:T(256)(128)(2,1)S(1)}, bf16[192]{0:T(256)(128)(2,1)}, u32[]{:S(2)}) copy-start(bf16[192]{0:T(256)(128)(2,1)} %param.28) | copy-start | bytes 1156
  45.8 48.4 %copy-start.18 = (bf16[48]{0:T(256)(128)(2,1)S(1)}, bf16[48]{0:T(256)(128)(2,1)}, u32[]{:S(2)}) copy-start(bf16[48]{0:T(256)(128)(2,1)} %param.29) | copy-start | bytes 292
  45.8 169.5 %all-to-all-start.2 = ((bf16[2,512,768]{2,1,0:T(8,128)(2,1)}), bf16[2,512,768]{2,1,0:T(8,128)(2,1)S(1)}, u32[]{:S(2)}, u32[]{:S(2)}) async-start(bf16[2,512,768]{2,1,0:T(8,128)(2,1)} %param.18), calls=%async_computation.2 | async-start | bytes 3145728 | tf_op jit(solution)/shard_map/all_to_all | solution.py:720
  49.6 443.7 %reduce-scatter.15.cloned.1.call-start = ((), (), s32[]{:S(2)}) async-start(), calls=%async_computation.21 | async-start | bytes 1253376 | tf_op jit(solution)/shard_map/reduce_scatter | solution.py:739
  215.3 81.6 %copy-start = (bf16[2,512,768]{2,1,0:T(8,128)(2,1)}, bf16[2,512,768]{2,1,0:T(8,128)(2,1)S(1)}, u32[]{:S(2)}) copy-start(bf16[2,512,768]{2,1,0:T(8,128)(2,1)S(1)} %all-to-all-done.2) | copy-start | bytes 4718596
  436.5 117.5 %reduce-scatter.19.cloned.1.call-start = ((), (), s32[]{:S(2)}) async-start(), calls=%async_computation.23 | async-start | bytes 1253376 | tf_op jit(solution)/shard_map/reduce_scatter | solution.py:739
  437.2 187.7 %reduce-scatter.13.cloned.1.call-start = ((), (), s32[]{:S(2)}) async-start(), calls=%async_computation.20 | async-start | bytes 3760128 | tf_op jit(solution)/shard_map/reduce_scatter | solution.py:739
  438.0 257.6 %reduce-scatter.17.cloned.1.call-start = ((), (), s32[]{:S(2)}) async-start(), calls=%async_computation.22 | async-start | bytes 3760128 | tf_op jit(solution)/shard_map/reduce_scatter | solution.py:739
  438.6 335.4 %reduce-scatter.21.cloned.1.call-start = ((), (), s32[]{:S(2)}) async-start(), calls=%async_computation.24 | async-start | bytes 5013504 | tf_op jit(solution)/shard_map/reduce_scatter | solution.py:739
  439.3 413.5 %reduce-scatter.23.cloned.1.call-start = ((), (), s32[]{:S(2)}) async-start(), calls=%async_computation.25 | async-start | bytes 5013504 | tf_op jit(solution)/shard_map/reduce_scatter | solution.py:739
  439.7 0.7 copy-start.9
  439.8 0.8 copy-start.8
  456.4 2.5 copy-start.2
  463.5 10.7 %all-to-all-start.5 = ((bf16[2,2,49152]{2,1,0:T(2,128)(2,1)}), bf16[2,2,49152]{2,1,0:T(2,128)(2,1)S(1)}, u32[]{:S(2)}, u32[]{:S(2)}) async-start(bf16[2,2,49152]{2,1,0:T(2,128)(2,1)} %reshape.85), calls=%async_computation.5 | async-start | bytes 786432 | tf_op jit(solution)/shard_map/all_to_all | solution.py:736
  467.0 11.9 %copy-start.7 = (f32[8,768]{1,0:T(8,128)S(1)}, f32[8,768]{1,0:T(8,128)}, u32[]{:S(2)}) copy-start(f32[8,768]{1,0:T(8,128)} %get-tuple-element.62) | copy-start | bytes 73732
  474.2 396.6 %all-to-all-start.4 = ((bf16[2,2,196608]{2,1,0:T(2,128)(2,1)}), bf16[2,2,196608]{2,1,0:T(2,128)(2,1)}, u32[]{:S(2)}, u32[]{:S(2)}) async-start(bf16[2,2,196608]{2,1,0:T(2,128)(2,1)} %reshape.83), calls=%async_computation.4 | async-start | bytes 3145728 | tf_op jit(solution)/shard_map/all_to_all | solution.py:736
  478.9 430.8 %reduce-scatter.25.cloned.1.call-start = ((), (), s32[]{:S(2)}) async-start(), calls=%async_computation.26 | async-start | bytes 208896
  479.9 486.4 %reduce-scatter.27.cloned.1.call-start = ((), (), s32[]{:S(2)}) async-start(), calls=%async_computation.27 | async-start | bytes 208896
  480.8 530.8 %all-reduce.10.cloned.1.call-start = ((), (), s32[]{:S(2)}) async-start(), calls=%async_computation.28 | async-start | bytes 2359296 | tf_op jit(solution)/shard_map/psum | solution.py:740
  870.8 6.1 copy-start.10
  870.8 109.1 %all-to-all-start.3 = ((bf16[2,2,196608]{2,1,0:T(2,128)(2,1)}), bf16[2,2,196608]{2,1,0:T(2,128)(2,1)}, u32[]{:S(2)}, u32[]{:S(2)}) async-start(bf16[2,2,196608]{2,1,0:T(2,128)(2,1)} %reshape.81), calls=%async_computation.3 | async-start | bytes 3145728 | tf_op jit(solution)/shard_map/all_to_all | solution.py:736
  1011.6 3.7 copy-start.4
  1011.6 4.5 copy-start.3
  1011.6 5.3 copy-start.6
  1011.6 6.0 copy-start.5
Sparse Core Ops, SparseCore 0:
  10.3 41.0 all-gather.10
  53.7 46.1 all-gather.8
  102.2 37.4 all-gather.14
  141.8 46.2 all-gather.12
  190.3 52.4 all-gather.16
  244.9 51.9 all-gather.18
  436.6 56.6 reduce-scatter.14
  496.9 57.0 reduce-scatter.18
  557.9 66.9 reduce-scatter.12
  628.6 66.9 reduce-scatter.16
  699.4 74.4 reduce-scatter.20
  778.2 74.6 reduce-scatter.22
  856.9 52.7 reduce-scatter.24
  913.6 52.6 reduce-scatter.26
  968.7 42.8 all-reduce.9
